TPU v7x, 32 devices: a whole 2x2x4 slice. The times are simulated.
32 devices in a mesh: fsdp: 32 (over z, y, x, core).
Axes of the slice: x: 2, y: 2, z: 4, core: 2. Of those that a mesh axis runs over, the one named last changes fastest.
Arguments:
- hidden: bfloat16 [32768, 768], P('fsdp'), may hold values from -6 to 6
- lengths: int32 [32], P('fsdp'), may hold values from 1 to 1024, 24576 in all
- norm_gain: bfloat16 [768], P('fsdp'), may hold values from 0.5 to 1.5
- in_w: bfloat16 [768, 3352], P('fsdp'), may hold values from -0.21875 to 0.21875
- conv_w: bfloat16 [4, 1792], P(None, 'fsdp'), may hold values from -3 to 3
- conv_b: bfloat16 [1792], P('fsdp'), may hold values from -3 to 3
- dt_bias: float32 [24], replicated, may hold values from -4 to 2
- a_log: float32 [24], replicated, may hold values from -5 to 2.5
- skip: float32 [24], replicated, may hold values from 0.5 to 1.5
- gate_gain: bfloat16 [1536], P('fsdp'), may hold values from 0.5 to 1.5
- out_w: bfloat16 [1536, 768], P('fsdp'), may hold values from -0.21875 to 0.21875
- cotangent: bfloat16 [32768, 768], P('fsdp'), may hold values from -6 to 6
Outputs:
- block_out: bfloat16 [32768, 768], P('fsdp')
- grad_hidden: float32 [32768, 768], P('fsdp')
- grad_norm_gain: float32 [768], P('fsdp')
- grad_in_w: float32 [768, 3352], P('fsdp')
- grad_conv_w: float32 [4, 1792], P(None, 'fsdp')
- grad_conv_b: float32 [1792], P('fsdp')
- grad_dt_bias: float32 [24], replicated
- grad_a_log: float32 [24], replicated
- grad_skip: float32 [24], replicated
- grad_gate_gain: float32 [1536], P('fsdp')
- grad_out_w: float32 [1536, 768], P('fsdp')
All inputs are finite; a program needn't handle non-finite values. No bound on the sum of `lengths` on one device may be relied on, other than what follows from the above.
Results may differ from a plain program's by a relative error of at most 0.0099.
Values may be sent and summed in bfloat16 or wider, within the bound.
No kernel may reach another device: no remote copies, remote signals or barrier semaphores. Data moves between devices by JAX's collectives and lax.ppermute only.
A program may use at most 192 MiB of HBM per device.

v0:
```python
import jax
import jax.numpy as jnp
from jax import lax
from jax.sharding import PartitionSpec as P

HEADS = 24
HEAD_DIM = 64
STATE = 128
CONV_K = 4
GROUP = 256


eps = 1e-05
precise = lax.Precision.HIGHEST


def rms_scale(values_in, gain_row):
    return (
        values_in
        * lax.rsqrt(jnp.mean(values_in * values_in, axis=-1, keepdims=True) + eps)
        * gain_row
    )


def front_piece(projected, conv_w, conv_b, dt_bias, a_log):
    length = projected.shape[0]
    inner_width = HEADS * HEAD_DIM
    channels = inner_width + 2 * STATE
    gate_z = projected[:, :inner_width]
    conv_in = projected[:, inner_width : inner_width + channels]
    dt_raw = projected[:, inner_width + channels :]
    padded = jnp.pad(conv_in, ((CONV_K - 1, 0), (0, 0)))
    conv_out = conv_b[None, :] + jnp.zeros((length, channels), jnp.float32)
    for offset in range(CONV_K):
        conv_out = conv_out + conv_w[offset][None, :] * padded[offset : offset + length]
    step_size = jax.nn.softplus(dt_raw + dt_bias[None, :])
    log_decay = -jnp.exp(a_log)[None, :] * step_size
    return (jax.nn.silu(conv_out), gate_z, step_size, log_decay)


def scan_heads(values, b_in, c_out, step_size, log_decay, skip):
    length = values.shape[0]
    blocks = length // GROUP
    value_rows = values.reshape(blocks, GROUP, HEADS, HEAD_DIM)
    key_rows = b_in.reshape(blocks, GROUP, STATE)
    read_rows = c_out.reshape(blocks, GROUP, STATE)
    step_rows = step_size.reshape(blocks, GROUP, HEADS)
    running = jnp.cumsum(log_decay.reshape(blocks, GROUP, HEADS), axis=1)
    places = jnp.arange(GROUP)
    causal = (places[:, None] >= places[None, :])[None, :, :, None]
    differ = running[:, :, None, :] - running[:, None, :, :]
    decays = jnp.exp(jnp.where(causal, differ, -jnp.inf))
    intersection = jnp.einsum("cqn,csn->cqs", read_rows, key_rows, precision=precise)
    mixing = intersection[..., None] * decays * step_rows[:, None, :, :]
    local_part = jnp.einsum("cqsh,cshp->cqhp", mixing, value_rows, precision=precise)
    to_end = jnp.exp(running[:, -1:, :] - running) * step_rows
    block_states = jnp.einsum("csn,csh,cshp->chpn", key_rows, to_end, value_rows, precision=precise)
    through = jnp.exp(running[:, -1, :])

    def carry_state(state_now, pieces):
        factor, fresh_state = pieces
        return (factor[:, None, None] * state_now + fresh_state, state_now)

    start = jnp.zeros((HEADS, HEAD_DIM, STATE), jnp.float32)
    _, entering = lax.scan(carry_state, start, (through, block_states))
    carried = jnp.einsum(
        "cqn,cqh,chpn->cqhp", read_rows, jnp.exp(running), entering, precision=precise
    )
    result = local_part + carried + skip[None, None, :, None] * value_rows
    return result.reshape(length, HEADS, HEAD_DIM)


def back_piece(mixed_low, gate_z, step_size, log_decay, skip, gate_gain):
    length = mixed_low.shape[0]
    inner_width = HEADS * HEAD_DIM
    values = mixed_low[:, :inner_width].reshape(length, HEADS, HEAD_DIM)
    b_in = mixed_low[:, inner_width : inner_width + STATE]
    c_out = mixed_low[:, inner_width + STATE :]
    ssd = scan_heads(values, b_in, c_out, step_size, log_decay, skip)
    gated = ssd.reshape(length, inner_width) * jax.nn.silu(gate_z)
    return rms_scale(gated, gate_gain)


def contract_rows(left, right):
    return lax.dot_general(
        left, right, (((0,), (0,)), ((), ())), preferred_element_type=jnp.float32
    )


def local(
    hidden,
    lengths,
    norm_gain,
    in_w,
    conv_w,
    conv_b,
    dt_bias,
    a_log,
    skip,
    gate_gain,
    out_w,
    cotangent,
):
    full_norm, full_in, full_conv, full_bias, full_gate, full_out = (
        lax.all_gather(norm_gain, "fsdp", axis=0, tiled=True),
        lax.all_gather(in_w, "fsdp", axis=0, tiled=True),
        lax.all_gather(conv_w, "fsdp", axis=1, tiled=True),
        lax.all_gather(conv_b, "fsdp", axis=0, tiled=True),
        lax.all_gather(gate_gain, "fsdp", axis=0, tiled=True),
        lax.all_gather(out_w, "fsdp", axis=0, tiled=True),
    )
    length = hidden.shape[0]
    inputs = hidden.astype(jnp.float32)
    keep_rows = (jnp.arange(length) < lengths[0]).astype(jnp.float32)[:, None]
    normed, norm_back = jax.vjp(rms_scale, inputs, full_norm.astype(jnp.float32))
    normed_low = normed.astype(jnp.bfloat16)
    projected = jnp.dot(normed_low, full_in, preferred_element_type=jnp.float32)
    front_outs, front_back = jax.vjp(
        front_piece,
        projected,
        full_conv.astype(jnp.float32),
        full_bias.astype(jnp.float32),
        dt_bias,
        a_log,
    )
    mixed, gate_z, step_size, log_decay = front_outs
    mixed_low = lax.optimization_barrier(mixed.astype(jnp.bfloat16)).astype(jnp.float32)
    normed_out, inner_back = jax.vjp(
        back_piece, mixed_low, gate_z, step_size, log_decay, skip, full_gate.astype(jnp.float32)
    )
    out_low = normed_out.astype(jnp.bfloat16)
    branch = jnp.dot(out_low, full_out, preferred_element_type=jnp.float32)
    block_out = (keep_rows * (inputs + branch)).astype(jnp.bfloat16)
    back_in, back_out = (
        lax.all_gather(in_w, "fsdp", axis=0, tiled=True),
        lax.all_gather(out_w, "fsdp", axis=0, tiled=True),
    )
    grad_rows = cotangent * keep_rows.astype(jnp.bfloat16)
    d_normed_out = lax.dot_general(
        grad_rows, back_out, (((1,), (1,)), ((), ())), preferred_element_type=jnp.float32
    )
    d_out_w = contract_rows(out_low, grad_rows)
    d_mixed, d_gate_z, d_step, d_log, d_skip, d_gate_gain = inner_back(d_normed_out)
    d_projected, d_conv_w, d_conv_b, d_dt_bias, d_a_log = front_back(
        (d_mixed, d_gate_z, d_step, d_log)
    )
    d_proj_low = d_projected.astype(jnp.bfloat16)
    d_normed = lax.dot_general(
        d_proj_low, back_in, (((1,), (1,)), ((), ())), preferred_element_type=jnp.float32
    )
    d_in_w = contract_rows(normed_low, d_proj_low)
    d_inputs, d_norm_gain = norm_back(d_normed)
    shares = (
        lax.psum_scatter(d_norm_gain, "fsdp", scatter_dimension=0, tiled=True),
        lax.psum_scatter(d_in_w, "fsdp", scatter_dimension=0, tiled=True),
        lax.psum_scatter(d_conv_w, "fsdp", scatter_dimension=1, tiled=True),
        lax.psum_scatter(d_conv_b, "fsdp", scatter_dimension=0, tiled=True),
        lax.psum_scatter(d_gate_gain, "fsdp", scatter_dimension=0, tiled=True),
        lax.psum_scatter(d_out_w, "fsdp", scatter_dimension=0, tiled=True),
    )
    grad_hidden = grad_rows.astype(jnp.float32) + d_inputs
    head_sums = lax.psum((d_dt_bias, d_a_log, d_skip), "fsdp")
    return (
        block_out,
        grad_hidden,
        shares[0],
        shares[1],
        shares[2],
        shares[3],
        head_sums[0],
        head_sums[1],
        head_sums[2],
        shares[4],
        shares[5],
    )


def solution(mesh):
    return jax.shard_map(
        local,
        mesh=mesh,
        in_specs=(
            P("fsdp", None),
            P("fsdp"),
            P("fsdp"),
            P("fsdp", None),
            P(None, "fsdp"),
            P("fsdp"),
            P(),
            P(),
            P(),
            P("fsdp"),
            P("fsdp", None),
            P("fsdp", None),
        ),
        out_specs=(
            P("fsdp", None),
            P("fsdp", None),
            P("fsdp"),
            P("fsdp", None),
            P(None, "fsdp"),
            P("fsdp"),
            P(),
            P(),
            P(),
            P("fsdp"),
            P("fsdp", None),
        ),
        check_vma=False,
    )
```

profile of v0, /device:TPU:0, one launch (start us, length us, event | category | flops | bytes accessed | tf_op | source)
XLA Modules:
  0.0 628.3 jit_solution(8035584218100557411)
XLA Ops:
  11.3 42.3 %all-reduce.26 = (bf16[768]{0:T(1024)(128)(2,1)S(1)}, bf16[1792]{0:T(1024)(128)(2,1)S(1)}, bf16[1536]{0:T(1024)(128)(2,1)S(1)}) all-reduce(bf16[768]{0:T(1024)(128)(2,1)S(1)} %dynamic-update-slice.1, bf16[1792]{0:T(1024)(128)(2,1)S(1)} %dynamic-update-slice, bf16[1536]{0:T(1024)(128)(2,1)S(1)} %dynamic-update-slice.2), channel_id=1, replica_groups=mesh['fsdp'=32] {'fsdp'}, use_global_device_ids=true, to_apply=%add.18 | all-reduce | flops 4096 | bytes 16384
  53.7 1.8 fusion.56
  56.2 40.9 %all-gather = bf16[32,56,4]{1,2,0:T(4,128)(2,1)S(1)} all-gather(bf16[1,56,4]{1,2,0:T(4,128)(2,1)} %bitcast.251), channel_id=1, replica_groups=mesh['fsdp'=32] {'fsdp'}, dimensions={0}, use_global_device_ids=true | all-gather | bytes 14784 | tf_op jit(solution)/shard_map/all_gather | solution.py:107
  98.0 8.6 %fusion.84 = f32[1024,3352]{0,1:T(8,128)S(1)} fusion(bf16[768,3352]{1,0:T(8,128)(2,1)} %all-gather.4.cloned.1.call-done, bf16[1024,768]{1,0:T(8,128)(2,1)} %param.16, f32[768]{0:T(1024)S(1)} %convert_element_type.58, f32[1024]{0:T(1024)S(1)} %fusion.95), kind=kOutput, calls=%fused_computation.127 | convolution fusion | flops 5275385856 | bytes 20458496 | tf_op jit(solution)/shard_map/dot_general | solution.py:117
  106.7 1.4 slice.80
  108.1 10.6 %multiply_convert_fusion = (bf16[1024,1792]{0,1:T(8,128)(2,1)}, f32[1024,1792]{0,1:T(8,128)}) fusion(f32[1024,1792]{0,1:T(8,128)S(1)} %slice.80, f32[1792]{0:T(1024)S(1)} %get-tuple-element.249, f32[1792]{0:T(1024)S(1)} %get-tuple-element.250, f32[1792]{0:T(1024)S(1)} %get-tuple-element.251, f32[1792]{0:T(1024)S(1)} %get-tuple-element.248, ...), kind=kLoop, calls=%fused_computation.51 | loop fusion | flops 23855104 | bytes 18385920 | tf_op jit(solution)/shard_map/convert_element_type | solution.py:127
  118.8 6.6 %slice_convert_fusion = (f32[1024,1536]{0,1:T(8,128)}, bf16[1024,1536]{0,1:T(8,128)(2,1)}) fusion(bf16[1024,1792]{0,1:T(8,128)(2,1)} %get-tuple-element.295), kind=kLoop, calls=%fused_computation.180 | loop fusion | flops 1572864 | bytes 12582912 | tf_op jit(solution)/shard_map/jvp()/slice | solution.py:76
  125.4 1.1 fusion.108
  126.6 2.3 reduce-window.14
  129.6 6.2 reshape.207
  136.2 6.9 %fusion.40 = f32[4,24,64,128]{3,2,1,0:T(8,128)} fusion(bf16[4,256,128,1]{2,1,3,0:T(8,128)(2,1)S(1)} %copy.249, f32[4,256,24]{1,2,0:T(8,128)S(1)} %get-tuple-element.314, bf16[4,256,24,64]{1,0,3,2:T(4,128)(2,1)} %reshape.207), kind=kOutput, calls=%fused_computation.80 | convolution fusion | flops 2419064832 | bytes 6651904 | tf_op jit(solution)/shard_map/jvp(csn,csh,cshp->chpn)/dot_general | solution.py:57
  143.1 2.1 broadcast.142.clone
  145.2 11.0 %while.34 = (s32[]{:T(128)}, f32[24,64,128]{2,1,0:T(8,128)S(1)}, f32[4,24,64,128]{3,2,1,0:T(8,128)}, f32[4,24,1,1]{1,3,2,0:T(1,128)}, f32[4,24]{1,0:T(4,128)S(1)...) while((s32[]{:T(128)}, f32[24,64,128]{2,1,0:T(8,128)S(1)}, f32[4,24,64,128]{3,2,1,0:T(8,128)}, ...), condition=%wide.region_4.5_spmd.clone, body=%wide.region_3.4_spmd.clone.sunk | while | flops 786435 | bytes 3934184 | solution.py:65
  145.2 0.9 bitcast_dynamic-update-slice_fusion.4
  146.1 1.3 bitcast_add_fusion.4
  147.9 0.9 bitcast_dynamic-update-slice_fusion.4
  148.9 1.3 bitcast_add_fusion.4
  151.6 1.3 bitcast_add_fusion.4
  154.3 1.3 bitcast_add_fusion.4
  157.1 8.1 %reshape.213 = f32[4,256,24,64]{1,0,3,2:T(4,128)} reshape(f32[1024,1536]{0,1:T(8,128)} %get-tuple-element.306) | data formatting | bytes 12582912 | tf_op jit(solution)/shard_map/jvp()/reshape;jvp()/reshape | solution.py:44
  165.5 5.1 fusion.110
  170.6 2.6 copy-done.10
  173.2 19.8 %fusion.36 = f32[4,256,24,64]{1,3,2,0:T(8,128)S(1)} fusion(f32[4,24,64,256]{3,2,1,0:T(8,128)S(1)} %fusion.110, f32[4,256,24,64]{1,0,3,2:T(4,128)S(1)} %copy-done.13, f32[24]{0:T(128)S(1)} %copy-done.53, f32[4,256,24]{1,2,0:T(8,128)S(1)} %get-tuple-element.313, f32[4,256,24]{1,2,0:T(8,128)S(1)} %bitcast.246, f32[4,256,24]{1,2,0:T(8,128)S(1)} %bitcast_bitcast_fusion.1, ...), kind=kOutput, calls=%fused_computation.67 | convolution fusion | flops 4863295488 | bytes 23429216 | tf_op jit(solution)/shard_map/jvp(cqsh,cshp->cqhp)/dot_general | solution.py:55
  193.0 5.0 copy.225
  198.0 1.5 copy.287
  199.6 7.9 %multiply_reduce_fusion.9 = (f32[1024]{0:T(1024)S(1)}, f32[1024,1536]{0,1:T(8,128)}) fusion(f32[1024,1536]{0,1:T(8,128)S(1)} %bitcast.223, f32[1024,3352]{0,1:T(8,128)} %copy-done.5), kind=kLoop, calls=%fused_computation.75 | loop fusion | flops 11009024 | bytes 18878464 | tf_op jit(solution)/shard_map/jvp()/reduce_sum | solution.py:20
  207.5 8.4 %multiply_reduce_fusion.6 = (f32[1536]{0:T(1024)}, f32[1024]{0:T(1024)S(1)}, f32[1024,1536]{0,1:T(8,128)S(1)}) fusion(f32[1024,1536]{0,1:T(8,128)} %get-tuple-element.294, f32[1024]{0:T(1024)S(1)} %fusion.96, f32[1536]{0:T(1024)S(1)} %convert_element_type.61, bf16[1536,768]{1,0:T(8,128)(2,1)} %all-gather.6.cloned.1.call-done, bf16[1024,768]{1,0:T(8,128)(2,1)} %param.27, ...), kind=kOutput, calls=%fused_computation.71 | convolution fusion | flops 2426140160 | bytes 16537600 | tf_op jit(solution)/shard_map/dot_general | solution.py:139
  216.1 10.3 %multiply_reduce_fusion.7 = (f32[1536]{0:T(1024)S(1)}, f32[1024,1536]{0,1:T(8,128)}, f32[1024,1536]{0,1:T(8,128)}) fusion(bf16[1024,1792]{0,1:T(8,128)(2,1)S(1)} %copy-done.6, f32[1024,3352]{0,1:T(8,128)} %copy-done.5, f32[1024,1536]{0,1:T(8,128)S(1)} %copy-done.11, f32[1024]{0:T(1024)S(1)} %multiply_multiply_fusion.2, f32[1024]{0:T(1024)S(1)} %fusion.96, ...), kind=kLoop, calls=%fused_computation.72 | loop fusion | flops 31455744 | bytes 40914944 | tf_op jit(solution)/shard_map/transpose(jvp())/reduce_sum | solution.py:69
  226.4 8.3 %reshape.215 = f32[4,256,24,64]{1,0,3,2:T(4,128)} reshape(f32[1024,1536]{0,1:T(8,128)} %get-tuple-element.289) | data formatting | bytes 12582912 | tf_op jit(solution)/shard_map/transpose(jvp())/reshape;transpose(jvp())/reshape | solution.py:70
  234.7 8.2 %fusion.33 = f32[4,24,64,128]{3,2,1,0:T(8,128)} fusion(bf16[4,256,128,1]{2,1,3,0:T(8,128)(2,1)S(1)} %copy.250, f32[4,256,24,64]{1,0,3,2:T(4,128)} %reshape.215, f32[4,256,24]{1,2,0:T(8,128)S(1)} %get-tuple-element.313), kind=kOutput, calls=%fused_computation.62 | convolution fusion | flops 2417491968 | bytes 9797632 | tf_op jit(solution)/shard_map/transpose(jvp(cqn,cqh,chpn->cqhp))/dot_general | solution.py:66
  243.0 5.5 fusion.37
  248.5 30.2 %fusion.11 = (f32[4,256,24]{1,2,0:T(8,128)}, f32[4,256,24]{1,2,0:T(8,128)}, f32[4,256,24]{1,2,0:T(8,128)}, f32[4,256,256]{2,1,0:T(8,128)S(1)}) fusion(f32[4,256,24]{1,2,0:T(8,128)S(1)} %bitcast.248, f32[4,256,24]{1,2,0:T(8,128)S(1)} %copy-done.25, f32[4,256,256]{2,1,0:T(8,128)S(1)} %copy-done.20, pred[256,256]{1,0:T(8,128)(4,1)S(1)} %copy-done.39, ...), kind=kOutput, calls=%fused_computation.22 | convolution fusion | flops 4913291264 | bytes 12091392 | tf_op jit(solution)/shard_map/transpose(jvp(cqsh,cshp->cqhp))/dot_general | solution.py:55
  278.8 11.0 %fusion.72 = f32[4,256,128]{2,1,0:T(8,128)} fusion(f32[4,24,64,128]{3,2,1,0:T(8,128)S(1)} %copy-done.2, f32[4,256,24,64]{1,0,3,2:T(4,128)S(1)} %copy-done, f32[4,256,24]{1,2,0:T(8,128)S(1)} %get-tuple-element.313), kind=kOutput, calls=%fused_computation.118 | convolution fusion | flops 2417491968 | bytes 10059776 | tf_op jit(solution)/shard_map/transpose(jvp(cqn,cqh,chpn->cqhp))/dot_general | solution.py:66
  289.8 2.1 broadcast.142
  291.9 13.4 %while.35 = (s32[]{:T(128)}, f32[24,64,128]{2,1,0:T(8,128)S(1)}, f32[4,24]{1,0:T(4,128)S(1)}, f32[4,24,64,128]{3,2,1,0:T(8,128)}, f32[4,24,64,128]{3,2,1,0:T(8,1...) while((s32[]{:T(128)}, f32[24,64,128]{2,1,0:T(8,128)S(1)}, ...), condition=%wide.region_9.10_spmd.clone, body=%wide.region_7.9_spmd.clone.sunk | while | flops 1179628 | bytes 4719308 | solution.py:65
  291.9 1.0 bitcast_dynamic-update-slice_fusion.5
  293.5 1.6 fusion.135
  295.2 1.0 bitcast_dynamic-update-slice_fusion.5
  296.9 1.6 fusion.135
  298.6 0.9 bitcast_dynamic-update-slice_fusion.5
  300.2 1.6 fusion.135
  301.9 0.9 bitcast_dynamic-update-slice_fusion.5
  303.5 1.6 fusion.135
  305.4 4.7 fusion.111
  310.1 11.0 %fusion.71 = f32[4,256,128]{2,1,0:T(8,128)} fusion(f32[4,24,64,128]{3,2,1,0:T(8,128)S(1)} %copy-done.12, f32[4,256,24]{1,2,0:T(8,128)S(1)} %copy-done.23, bf16[4,256,24,64]{1,0,3,2:T(4,128)(2,1)S(1)} %copy-done.9), kind=kOutput, calls=%fused_computation.117 | convolution fusion | flops 2419064832 | bytes 6914048 | tf_op jit(solution)/shard_map/transpose(jvp(csn,csh,cshp->chpn))/dot_general | solution.py:57
  321.2 6.2 multiply_reduce_fusion.5
  327.4 25.6 %bitcast_add_fusion.2 = f32[4,256,24,64]{1,3,2,0:T(8,128)} fusion(f32[4,256,24,64]{1,3,2,0:T(8,128)S(1)} %fusion.111, f32[4,256,24,64]{1,0,3,2:T(4,128)S(1)} %bitcast.220, f32[4,256,24]{1,2,0:T(8,128)} %bitcast.247, f32[4,256,24]{1,2,0:T(8,128)S(1)} %copy-done.26, f32[4,256,256]{2,1,0:T(8,128)} %copy-done.19, pred[256,256]{1,0:T(8,128)(4,1)S(1)} %copy-done.40, ...), kind=kOutput, calls=%fused_computation.56 | convolution fusion | flops 4863295488 | bytes 20283488 | tf_op jit(solution)/shard_map/transpose(jvp(cqsh,cshp->cqhp))/dot_general | solution.py:55
  353.0 4.7 fusion.75
  358.2 1.1 add_bitcast_fusion.1
  359.3 10.0 %reduce-window.16 = f32[4,24,2,128]{3,1,2,0:T(8,128)S(1)} reduce-window(f32[4,24,2,128]{3,1,2,0:T(8,128)S(1)} %bitcast.241, f32[]{:T(128)} %constant.95.clone.1), window={size=1x1x1x128 pad=0_0x0_0x0_0x0_127}, to_apply=%region_14.15 | reduce-window | flops 3121152 | bytes 196612 | tf_op jit(solution)/shard_map/reduce-window.2
  370.4 1.0 copy.275
  371.4 2.1 convolution_add_fusion
  373.7 8.1 %copy.247 = f32[4,256,24,64]{1,0,3,2:T(4,128)S(1)} copy(f32[4,256,24,64]{1,3,2,0:T(8,128)} %bitcast_add_fusion.2) | data formatting | bytes 12582912 | tf_op jit(solution)/shard_map/transpose(jvp(cqsh,cshp->cqhp))/add_any | solution.py:55
  381.8 1.6 copy.288
  383.5 2.0 fusion.104
  385.5 12.3 %multiply_reduce_fusion.3 = (f32[1792]{0:T(1024)S(1)}, f32[1792]{0:T(1024)S(1)}, f32[1792]{0:T(1024)S(1)}, f32[1792]{0:T(1024)S(1)}, f32[1792]{0:T(1024)S(1)}, /*index=5*/f32[1024,1792]{0,1:T(8,128)S(1)}) fusion(f32[1024,1792]{0,1:T(8,128)S(1)} %bitcast.222, f32[1024,3352]{0,1:T(8,128)} %copy-done.5, f32[1024,1792]{0,1:T(8,128)S(1)} %bitcast.226, ...), kind=kLoop, calls=%fused_computation.49 | loop fusion | flops 36691200 | bytes 36736000 | tf_op jit(solution)/shard_map/transpose(jvp())/reduce_sum | solution.py:35
  397.8 8.6 %broadcast_multiply_fusion = (f32[1024,1792]{0,1:T(8,128)S(1)}, f32[1024,1792]{0,1:T(8,128)}, f32[1024,1792]{0,1:T(8,128)}, f32[1024,1792]{0,1:T(8,128)}) fusion(f32[1024,1792]{0,1:T(8,128)S(1)} %get-tuple-element.292, f32[1792]{0:T(1024)S(1)} %copy-done.33, f32[1792]{0:T(1024)S(1)} %copy-done.31, f32[1792]{0:T(1024)S(1)} %copy-done.37, f32[1792]{0:T(1024)S(1)} %copy-done.35), kind=kLoop, calls=%fused_computation.95 | loop fusion | flops 7340032 | bytes 36728832 | tf_op jit(solution)/shard_map/transpose(jvp())/mul | solution.py:35
  406.4 12.3 %pad_add_fusion = f32[1024,1792]{0,1:T(8,128)} fusion(f32[1024,1792]{0,1:T(8,128)} %get-tuple-element.303, f32[1024,1792]{0,1:T(8,128)} %get-tuple-element.304, f32[1024,1792]{0,1:T(8,128)} %get-tuple-element.305, f32[1024,1792]{0,1:T(8,128)S(1)} %get-tuple-element.302), kind=kLoop, calls=%fused_computation.44 | loop fusion | flops 5505024 | bytes 36700160 | tf_op jit(solution)/shard_map/transpose(jvp())/add_any | solution.py:35
  418.8 15.2 %fusion.82 = f32[768,3352]{1,0:T(8,128)} fusion(bf16[1024,768]{1,0:T(8,128)(2,1)S(1)} %copy-done.14, f32[768]{0:T(1024)S(1)} %copy-done.44, f32[1024]{0:T(1024)S(1)} %copy-done.46, f32[1024,1536]{0,1:T(8,128)} %get-tuple-element.301, f32[1024,1792]{0,1:T(8,128)} %pad_add_fusion, f32[1024,24]{0,1:T(8,128)S(1)} %get-tuple-element.291), kind=kOutput, calls=%fused_computation.126 | convolution fusion | flops 5285683200 | bytes 25607168 | tf_op jit(solution)/shard_map/dot_general | solution.py:85
  434.7 12.7 %fusion.54 = (f32[768]{0:T(1024)S(1)}, f32[1024]{0:T(1024)S(1)}, f32[1024,768]{1,0:T(8,128)}) fusion(bf16[1024,768]{1,0:T(8,128)(2,1)S(1)} %copy-done.14, f32[1024]{0:T(1024)S(1)} %copy-done.46, f32[768]{0:T(1024)S(1)} %copy-done.44, bf16[768,3352]{1,0:T(8,128)(2,1)} %all-gather.4.cloned.1.call-done, f32[1024,1536]{0,1:T(8,128)} %get-tuple-element.301, ...), kind=kOutput, calls=%fused_computation.100 | convolution fusion | flops 5288040448 | bytes 23611392 | tf_op jit(solution)/shard_map/dot_general | solution.py:148
  447.4 38.0 %all-reduce.25 = (f32[768]{0:T(1024)S(1)}, f32[4,1792]{1,0:T(4,128)S(1)}, f32[1792]{0:T(1024)S(1)}, f32[24]{0:T(128)}, f32[24]{0:T(128)}, /*index=5*/f32[24]{0:T(128)}, f32[1536]{0:T(1024)S(1)}) all-reduce(f32[768]{0:T(1024)S(1)} %get-tuple-element.246, f32[4,1792]{1,0:T(4,128)S(1)} %pad_add_fusion.3, ...), channel_id=2, replica_groups=mesh['fsdp'=32] {'fsdp'}, use_global_device_ids=true, to_apply=%region_19.20.clone | all-reduce | flops 11336 | bytes 90688
  487.9 3.8 fusion.55
  491.8 7.3 %fusion.58 = bf16[1024,768]{1,0:T(8,128)(2,1)} fusion(bf16[1024,768]{1,0:T(8,128)(2,1)S(1)} %copy-done.14, bf16[1536,768]{1,0:T(8,128)(2,1)S(1)} %copy-done.52, f32[1024]{0:T(1024)S(1)} %fusion.94, f32[1024,1536]{0,1:T(8,128)} %get-tuple-element.294, f32[1536]{0:T(1024)S(1)} %convert_element_type.61, f32[1024]{0:T(1024)S(1)} %fusion.96), kind=kOutput, calls=%fused_computation.104 | convolution fusion | flops 2423783424 | bytes 11810816 | tf_op jit(solution)/shard_map/dot_general | solution.py:132
  499.0 122.3 %reduce-scatter.8.cloned.1.call-done = f32[24,3352]{1,0:T(8,128)} async-done(((f32[768,3352]{1,0:T(8,128)}), f32[24,3352]{1,0:T(8,128)}) %reduce-scatter.8.cloned.1.call-update) | async-done | bytes 321808
  (227 shorter events, 19.3 us)
Async XLA Ops:
  7.2 90.9 %all-gather.4.cloned.1.call-start = ((), (), s32[]{:S(2)}) async-start(), calls=%async_computation.2 | async-start | bytes 5474304 | tf_op jit(solution)/shard_map/all_gather | solution.py:106
  7.9 199.6 %all-gather.6.cloned.1.call-start = ((), (), s32[]{:S(2)}) async-start(), calls=%async_computation.3 | async-start | bytes 2433024 | tf_op jit(solution)/shard_map/all_gather | solution.py:110
  8.7 490.4 %reduce-scatter.6.cloned.1.call-start = ((), (), s32[]{:S(2)}) async-start(), calls=%async_computation.4 | async-start | bytes 4866048 | tf_op jit(solution)/shard_map/reduce_scatter | solution.py:159
  8.8 161.8 %copy-start.38 = (pred[256,256]{1,0:T(8,128)(4,1)}, pred[256,256]{1,0:T(8,128)(4,1)S(1)}, u32[]{:S(2)}) copy-start(pred[256,256]{1,0:T(8,128)(4,1)S(1)} %iota_compare_fusion) | copy-start | bytes 196612
  53.7 53.0 %copy-start.43 = (f32[768]{0:T(1024)}, f32[768]{0:T(1024)S(1)}, u32[]{:S(2)}) copy-start(f32[768]{0:T(1024)S(1)} %convert_element_type.58) | copy-start | bytes 9220
  55.5 51.2 %copy-start.45 = (f32[1024]{0:T(1024)}, f32[1024]{0:T(1024)S(1)}, u32[]{:S(2)}) copy-start(f32[1024]{0:T(1024)S(1)} %fusion.95) | copy-start | bytes 12292
  56.2 70.3 %copy-start.50 = (f32[24]{0:T(128)}, f32[24]{0:T(128)S(1)}, u32[]{:S(2)}) copy-start(f32[24]{0:T(128)S(1)} %exponential_negate_fusion) | copy-start | bytes 292
  97.3 10.8 %copy-start.30 = (f32[1792]{0:T(1024)}, f32[1792]{0:T(1024)S(1)}, u32[]{:S(2)}) copy-start(f32[1792]{0:T(1024)S(1)} %get-tuple-element.248) | copy-start | bytes 21508
  97.3 10.8 %copy-start.32 = (f32[1792]{0:T(1024)}, f32[1792]{0:T(1024)S(1)}, u32[]{:S(2)}) copy-start(f32[1792]{0:T(1024)S(1)} %get-tuple-element.249) | copy-start | bytes 21508
  97.3 10.8 %copy-start.34 = (f32[1792]{0:T(1024)}, f32[1792]{0:T(1024)S(1)}, u32[]{:S(2)}) copy-start(f32[1792]{0:T(1024)S(1)} %get-tuple-element.250) | copy-start | bytes 21508
  97.3 10.8 %copy-start.36 = (f32[1792]{0:T(1024)}, f32[1792]{0:T(1024)S(1)}, u32[]{:S(2)}) copy-start(f32[1792]{0:T(1024)S(1)} %get-tuple-element.251) | copy-start | bytes 21508
  106.7 19.7 %copy-start.5 = (f32[1024,3352]{0,1:T(8,128)}, f32[1024,3352]{0,1:T(8,128)S(1)}, u32[]{:S(2)}) copy-start(f32[1024,3352]{0,1:T(8,128)S(1)} %fusion.84) | copy-start | bytes 41189380
  108.1 10.7 %copy-start.1 = (f32[1024,1792]{0,1:T(8,128)}, f32[1024,1792]{0,1:T(8,128)S(1)}, u32[]{:S(2)}) copy-start(f32[1024,1792]{0,1:T(8,128)S(1)} %slice.80) | copy-start | bytes 22020100
  118.8 7.7 %copy-start.48 = (f32[24]{0:T(128)S(1)}, f32[24]{0:T(128)}, u32[]{:S(2)}) copy-start(f32[24]{0:T(128)} %param.22) | copy-start | bytes 292
  129.3 41.4 %copy-start.24 = (f32[4,256,24]{1,2,0:T(8,128)}, f32[4,256,24]{1,2,0:T(8,128)S(1)}, u32[]{:S(2)}) copy-start(f32[4,256,24]{1,2,0:T(8,128)S(1)} %bitcast_bitcast_fusion.1) | copy-start | bytes 294916
  129.6 13.5 %copy-start.22 = (f32[4,256,24]{1,2,0:T(8,128)}, f32[4,256,24]{1,2,0:T(8,128)S(1)}, u32[]{:S(2)}) copy-start(f32[4,256,24]{1,2,0:T(8,128)S(1)} %get-tuple-element.314) | copy-start | bytes 294916
  156.4 14.2 %copy-start.27 = (f32[3,4,8,256]{3,2,0,1:T(8,128)}, f32[3,4,8,256]{3,2,0,1:T(8,128)S(1)}, u32[]{:S(2)}) copy-start(f32[3,4,8,256]{3,2,0,1:T(8,128)S(1)} %copy.366) | copy-start | bytes 294916
  165.2 8.1 %copy-start.7 = (bf16[4,256,24,64]{1,0,3,2:T(4,128)(2,1)S(1)}, bf16[4,256,24,64]{1,0,3,2:T(4,128)(2,1)}, u32[]{:S(2)}) copy-start(bf16[4,256,24,64]{1,0,3,2:T(4,128)(2,1)} %reshape.207) | copy-start | bytes 9437188
  165.2 8.1 %copy-start.13 = (f32[4,256,24,64]{1,0,3,2:T(4,128)S(1)}, f32[4,256,24,64]{1,0,3,2:T(4,128)}, u32[]{:S(2)}) copy-start(f32[4,256,24,64]{1,0,3,2:T(4,128)} %reshape.213) | copy-start | bytes 18874372
  165.2 8.1 %copy-start.53 = (f32[24]{0:T(128)S(1)}, f32[24]{0:T(128)}, u32[]{:S(2)}) copy-start(f32[24]{0:T(128)} %param.24) | copy-start | bytes 292
  165.5 27.5 %copy-start.19 = (f32[4,256,256]{2,1,0:T(8,128)}, f32[4,256,256]{2,1,0:T(8,128)S(1)}, u32[]{:S(2)}) copy-start(f32[4,256,256]{2,1,0:T(8,128)S(1)} %fusion.109) | copy-start | bytes 3145732
  170.6 2.6 copy-start.10
  199.5 7.9 %copy-start.3 = (f32[192,8,4,256]{3,1,2,0:T(8,128)}, f32[192,8,4,256]{3,1,2,0:T(8,128)S(1)}, u32[]{:S(2)}) copy-start(f32[192,8,4,256]{3,1,2,0:T(8,128)S(1)} %copy.287) | copy-start | bytes 18874372
  207.5 8.4 %copy-start.4 = (f32[192,8,4,256]{3,1,2,0:T(8,128)S(1)}, f32[192,8,4,256]{3,1,2,0:T(8,128)}, u32[]{:S(2)}) copy-start(f32[192,8,4,256]{3,1,2,0:T(8,128)} %copy-done.3) | copy-start | bytes 18874372
  207.5 8.4 %copy-start.6 = (bf16[1024,1792]{0,1:T(8,128)(2,1)S(1)}, bf16[1024,1792]{0,1:T(8,128)(2,1)}, u32[]{:S(2)}) copy-start(bf16[1024,1792]{0,1:T(8,128)(2,1)} %get-tuple-element.295) | copy-start | bytes 11010052
  207.5 8.6 %copy-start.11 = (f32[1024,1536]{0,1:T(8,128)S(1)}, f32[1024,1536]{0,1:T(8,128)}, u32[]{:S(2)}) copy-start(f32[1024,1536]{0,1:T(8,128)} %get-tuple-element.294) | copy-start | bytes 18874372
  234.7 8.2 %copy-start = (f32[4,256,24,64]{1,0,3,2:T(4,128)S(1)}, f32[4,256,24,64]{1,0,3,2:T(4,128)}, u32[]{:S(2)}) copy-start(f32[4,256,24,64]{1,0,3,2:T(4,128)} %reshape.215) | copy-start | bytes 18874372
  242.9 5.6 copy-start.8
  242.9 5.6 copy-start.20
  242.9 5.6 copy-start.25
  242.9 5.6 copy-start.28
  242.9 5.6 copy-start.39
  248.5 30.2 %copy-start.2 = (f32[4,24,64,128]{3,2,1,0:T(8,128)S(1)}, f32[4,24,64,128]{3,2,1,0:T(8,128)}, u32[]{:S(2)}) copy-start(f32[4,24,64,128]{3,2,1,0:T(8,128)} %get-tuple-element.431) | copy-start | bytes 9437188
  305.3 4.8 copy-start.9
  305.3 4.8 copy-start.12
  305.3 4.8 copy-start.23
  310.1 17.2 %slice-start = ((s8[6291456]{0:T(1024)(128)(4,1)}), s8[4194304]{0:T(1024)(128)(4,1)S(1)}, s32[]{:S(2)}) async-start(s8[6291456]{0:T(1024)(128)(4,1)} %bitcast.219), calls=%async_computation.6 | async-start | bytes 8388608
  321.2 6.2 slice-start.1
  321.2 6.2 copy-start.26
  321.2 6.2 copy-start.40
  321.2 31.8 %slice-start.6 = ((s8[6291456]{0:T(1024)(128)(4,1)}), s8[4194304]{0:T(1024)(128)(4,1)S(1)}, s32[]{:S(2)}) async-start(s8[6291456]{0:T(1024)(128)(4,1)} %bitcast.229), calls=%async_computation.12 | async-start | bytes 8388608
  327.4 25.6 %slice-start.7 = ((s8[6291456]{0:T(1024)(128)(4,1)}), s8[2097152]{0:T(1024)(128)(4,1)S(1)}, s32[]{:S(2)}) async-start(s8[6291456]{0:T(1024)(128)(4,1)} %bitcast.229), calls=%async_computation.13 | async-start | bytes 4194304
  327.4 25.6 %copy-start.17 = (bf16[1024,768]{1,0:T(8,128)(2,1)S(1)}, bf16[1024,768]{1,0:T(8,128)(2,1)}, u32[]{:S(2)}) copy-start(bf16[1024,768]{1,0:T(8,128)(2,1)} %param.27) | copy-start | bytes 4718596
  353.0 5.2 copy-start.21
  353.0 5.2 copy-start.29
  357.7 11.9 %copy-start.16 = (f32[4,256,128]{2,1,0:T(8,128)S(1)}, f32[4,256,128]{2,1,0:T(8,128)}, u32[]{:S(2)}) copy-start(f32[4,256,128]{2,1,0:T(8,128)} %fusion.72) | copy-start | bytes 1572868
  369.4 252.0 %reduce-scatter.8.cloned.1.call-start = ((), (), s32[]{:S(2)}) async-start(), calls=%async_computation.5 | async-start | bytes 10948608
  373.7 11.7 %slice-start.2 = ((s8[7340032]{0:T(1024)(128)(4,1)}), s8[3145728]{0:T(1024)(128)(4,1)S(1)}, s32[]{:S(2)}) async-start(s8[7340032]{0:T(1024)(128)(4,1)} %bitcast.221), calls=%async_computation.8 | async-start | bytes 6291456
  373.7 11.7 %slice-start.4 = ((s8[7340032]{0:T(1024)(128)(4,1)}), s8[4194304]{0:T(1024)(128)(4,1)S(1)}, s32[]{:S(2)}) async-start(s8[7340032]{0:T(1024)(128)(4,1)} %bitcast.225), calls=%async_computation.10 | async-start | bytes 8388608
  381.8 1.7 copy-start.49
  381.8 3.6 slice-start.3
  381.8 3.6 slice-start.5
  381.8 3.6 copy-start.15
  385.5 12.3 %copy-start.31 = (f32[1792]{0:T(1024)S(1)}, f32[1792]{0:T(1024)}, u32[]{:S(2)}) copy-start(f32[1792]{0:T(1024)} %copy-done.30) | copy-start | bytes 21508
  385.5 12.3 %copy-start.33 = (f32[1792]{0:T(1024)S(1)}, f32[1792]{0:T(1024)}, u32[]{:S(2)}) copy-start(f32[1792]{0:T(1024)} %copy-done.32) | copy-start | bytes 21508
  385.5 12.3 %copy-start.35 = (f32[1792]{0:T(1024)S(1)}, f32[1792]{0:T(1024)}, u32[]{:S(2)}) copy-start(f32[1792]{0:T(1024)} %copy-done.34) | copy-start | bytes 21508
  385.5 12.3 %copy-start.37 = (f32[1792]{0:T(1024)S(1)}, f32[1792]{0:T(1024)}, u32[]{:S(2)}) copy-start(f32[1792]{0:T(1024)} %copy-done.36) | copy-start | bytes 21508
  406.4 12.3 %copy-start.14 = (bf16[1024,768]{1,0:T(8,128)(2,1)S(1)}, bf16[1024,768]{1,0:T(8,128)(2,1)}, u32[]{:S(2)}) copy-start(bf16[1024,768]{1,0:T(8,128)(2,1)} %param.16) | copy-start | bytes 4718596
  406.4 12.3 %copy-start.44 = (f32[768]{0:T(1024)S(1)}, f32[768]{0:T(1024)}, u32[]{:S(2)}) copy-start(f32[768]{0:T(1024)} %copy-done.43) | copy-start | bytes 9220
  406.4 12.3 %copy-start.46 = (f32[1024]{0:T(1024)S(1)}, f32[1024]{0:T(1024)}, u32[]{:S(2)}) copy-start(f32[1024]{0:T(1024)} %copy-done.45) | copy-start | bytes 12292
  434.7 12.8 %copy-start.47 = (f32[1536]{0:T(1024)S(1)}, f32[1536]{0:T(1024)}, u32[]{:S(2)}) copy-start(f32[1536]{0:T(1024)} %get-tuple-element.242) | copy-start | bytes 18436
  434.7 53.2 %copy-start.42 = (f32[1024]{0:T(1024)S(1)}, f32[1024]{0:T(1024)}, u32[]{:S(2)}) copy-start(f32[1024]{0:T(1024)} %copy-done.41) | copy-start | bytes 12292
  434.7 53.2 %copy-start.18 = (bf16[1024,768]{1,0:T(8,128)(2,1)S(1)}, bf16[1024,768]{1,0:T(8,128)(2,1)}, u32[]{:S(2)}) copy-start(bf16[1024,768]{1,0:T(8,128)(2,1)} %param.27) | copy-start | bytes 4718596
  485.5 6.3 %copy-start.52 = (bf16[1536,768]{1,0:T(8,128)(2,1)S(1)}, bf16[1536,768]{1,0:T(8,128)(2,1)}, u32[]{:S(2)}) copy-start(bf16[1536,768]{1,0:T(8,128)(2,1)} %all-gather.6.cloned.1.call-done) | copy-start | bytes 7077892
  (3 other events, 3.0 us)
Sparse Core Ops, SparseCore 0:
  10.9 68.3 all-gather.3
  82.2 56.1 all-gather.5
  369.5 103.0 reduce-scatter.5
  480.2 141.0 reduce-scatter.7
where the time goes:
time: 636 us; the launch traced here: 628 us
  matrix products  182 us (29%)
  waiting for transfers between devices  124 us (19%)
  other arithmetic  122 us (19%)
  blocking collectives  121 us (19%)
  local copies, waits for them, and re-layouts  62.1 us (10%)
  between operations  16 us (3%)
    unnamed x5, waiting for transfers between devices  124 us
    unnamed x2, blocking collectives  80.4 us
    dot_general x3, matrix products, scan_heads(): jnp.einsum('cqsh,cshp->cqhp', mixing, value_rows, precision=precise)  75.5 us
    all_gather x1, blocking collectives, local(): lax.all_gather(conv_w, 'fsdp', axis=1, tiled=True)  40.9 us
    dot_general x3, matrix products, scan_heads(): jnp.einsum('cqn,cqh,chpn->cqhp', read_rows, jnp.exp(running), entering, p...  24.4 us
    dot_general x3, matrix products, scan_heads(): jnp.einsum('csn,csh,cshp->chpn', key_rows, to_end, value_rows, precision=...  22.7 us
    dot_general x2, matrix products, contract_rows(): lax.dot_general(left, right, (((0,), (0,)), ((), ())), preferred_element_...  19.9 us
    reshape x2, local copies, waits for them, and re-layouts, scan_heads(): value_rows = values.reshape(blocks, GROUP, HEADS, HEAD_DIM)  14.3 us
  transfers between devices with their start and end apart: 4, of which 1 were waited for; matrix products, arithmetic and copies ran while one was open for 32% of the time, Pallas kernels for 0%

commit v1 on v0

v1 whole, which is shorter than its diff:
```python
import functools

import jax
import jax.numpy as jnp
from jax import lax
from jax.experimental import pallas as pl
from jax.experimental.pallas import tpu as pltpu
from jax.sharding import PartitionSpec as P

HEADS = 24
HEAD_DIM = 64
STATE = 128
CONV_K = 4
INNER = HEADS * HEAD_DIM
CHANNELS = INNER + 2 * STATE
LANES = 128
CHUNK = 128
PAIRS = HEADS // 2
VMEM_BYTES = 56 * 1024 * 1024
EPS = 1e-05
F32 = jnp.float32
BF16 = jnp.bfloat16
HIGHEST = lax.Precision.HIGHEST


def mm(a, b):
    return lax.dot_general(a, b, (((1,), (0,)), ((), ())), preferred_element_type=F32)


def mm_bt(a, b):
    return lax.dot_general(a, b, (((1,), (1,)), ((), ())), preferred_element_type=F32)


def mm_at(a, b):
    return lax.dot_general(a, b, (((0,), (0,)), ((), ())), preferred_element_type=F32)


def sigmoid(x):
    return 0.5 * jnp.tanh(0.5 * x) + 0.5


def split_two(v):
    high = v.astype(BF16)
    low = (v - high.astype(F32)).astype(BF16)
    return high, low


def widen(v, spread):
    high, low = split_two(jnp.where(lane_is_head(), v, 0.0))
    packed = high.astype(F32) + pltpu.roll(low.astype(F32), 64, 1)
    return mm(packed.astype(BF16), spread)


def head_sums(v, gather):
    high, low = split_two(v)
    return mm(high, gather) + mm(low, gather)


def lane_is_head():
    return lax.broadcasted_iota(jnp.int32, (1, LANES), 1) < HEADS


def triangle(kind):
    rows = lax.broadcasted_iota(jnp.int32, (CHUNK, CHUNK), 0)
    columns = lax.broadcasted_iota(jnp.int32, (CHUNK, CHUNK), 1)
    return rows >= columns if kind == "lower" else rows <= columns


def forward_kernel(
    hidden_ref, gain_ref, wc_ref, wdt_ref, cw_ref, cb_ref, dtb_ref, alog_ref, skip_ref, spread_ref,
    normed_ref, mixed_ref, slope_ref, convin_ref, step_ref, run_ref, sig_ref, ssd_ref, enter_ref,
    tail, state,
):
    first = pl.program_id(0) == 0

    @pl.when(first)
    def _():
        tail[0:8, :] = jnp.zeros((8, CHANNELS), F32)
        state[...] = jnp.zeros_like(state)

    x = hidden_ref[...].astype(F32)
    scale = lax.rsqrt(jnp.mean(x * x, axis=-1, keepdims=True) + EPS)
    normed = (x * scale * gain_ref[...]).astype(BF16)
    normed_ref[...] = normed

    conv_in = mm(normed, wc_ref[...])
    convin_ref[...] = conv_in.astype(BF16)
    tail[8 : 8 + CHUNK, :] = conv_in
    conv_out = cb_ref[...] + cw_ref[3:4, :] * conv_in
    for k in range(CONV_K - 1):
        conv_out = conv_out + cw_ref[k : k + 1, :] * tail[5 + k : 5 + k + CHUNK, :]
    tail[0:8, :] = tail[CHUNK : CHUNK + 8, :]
    gate = sigmoid(conv_out)
    mixed = (conv_out * gate).astype(BF16)
    mixed_ref[...] = mixed
    slope_ref[...] = (gate * (1.0 + conv_out * (1.0 - gate))).astype(BF16)

    dt = mm(normed, wdt_ref[...]) + dtb_ref[...]
    step = jnp.where(lane_is_head(), jnp.maximum(dt, 0.0) + jnp.log1p(jnp.exp(-jnp.abs(dt))), 0.0)
    step_ref[...] = step
    sig_ref[...] = sigmoid(dt)
    log_decay = -jnp.exp(alog_ref[...]) * step
    lower = triangle("lower")
    run = jnp.dot(lower.astype(F32), log_decay, precision=HIGHEST, preferred_element_type=F32)
    run_ref[...] = run
    run_t = jnp.transpose(run)
    last = run[CHUNK - 1 : CHUNK, :]

    spread = spread_ref[...]
    values = mixed[:, :INNER].astype(F32)
    b_in = mixed[:, INNER : INNER + STATE]
    c_out = mixed[:, INNER + STATE :]
    scores = jnp.where(lower, mm_bt(c_out, b_in), 0.0)
    stepped = (widen(step, spread) * values).astype(BF16)
    entering = state[...]
    enter_low = entering.astype(BF16)
    enter_ref[0] = enter_low
    ssd_ref[...] = widen(jnp.exp(run), spread) * mm(c_out, enter_low) + skip_ref[...] * values
    to_end = (widen(jnp.exp(last - run), spread) * stepped.astype(F32)).astype(BF16)
    through = widen(jnp.broadcast_to(jnp.exp(last), (8, LANES)), spread)[0:1, :]
    state[...] = through * entering + mm_at(b_in, to_end)

    left_half = lax.broadcasted_iota(jnp.int32, (CHUNK, LANES), 1) < HEAD_DIM
    zero = jnp.zeros((CHUNK, LANES), BF16)
    for pair in range(PAIRS):
        mixing = []
        for h in (2 * pair, 2 * pair + 1):
            decay = jnp.exp(jnp.minimum(run[:, h : h + 1] - run_t[h : h + 1, :], 0.0))
            mixing.append((scores * decay).astype(BF16))
        both = stepped[:, pair * LANES : (pair + 1) * LANES]
        right = jnp.concatenate([jnp.where(left_half, both, zero), jnp.where(left_half, zero, both)], axis=0)
        ssd_ref[:, pair * LANES : (pair + 1) * LANES] += mm(jnp.concatenate(mixing, axis=1), right)


def forward(hidden, gain, wc, wdt, cw, cb, dtb, alog, skip_wide, spread):
    rows, width = hidden.shape
    chunks = rows // CHUNK
    whole = lambda a: pl.BlockSpec(a.shape, lambda i: (0,) * a.ndim)
    part = lambda n: pl.BlockSpec((CHUNK, n), lambda i: (i, 0))
    ins = (hidden, gain, wc, wdt, cw, cb, dtb, alog, skip_wide, spread)
    flops = 2 * rows * (width * (CHANNELS + LANES) + 3 * STATE * INNER + CHUNK * INNER * 2)
    return pl.pallas_call(
        forward_kernel,
        grid=(chunks,),
        in_specs=[part(width)] + [whole(a) for a in ins[1:]],
        out_specs=[
            part(width), part(CHANNELS), part(CHANNELS), part(CHANNELS), part(LANES), part(LANES), part(LANES), part(INNER),
            pl.BlockSpec((1, STATE, INNER), lambda i: (i, 0, 0)),
        ],
        out_shape=[
            jax.ShapeDtypeStruct((rows, width), BF16),
            jax.ShapeDtypeStruct((rows, CHANNELS), BF16),
            jax.ShapeDtypeStruct((rows, CHANNELS), BF16),
            jax.ShapeDtypeStruct((rows, CHANNELS), BF16),
            jax.ShapeDtypeStruct((rows, LANES), F32),
            jax.ShapeDtypeStruct((rows, LANES), F32),
            jax.ShapeDtypeStruct((rows, LANES), F32),
            jax.ShapeDtypeStruct((rows, INNER), F32),
            jax.ShapeDtypeStruct((chunks, STATE, INNER), BF16),
        ],
        scratch_shapes=[pltpu.VMEM((CHUNK + 8, CHANNELS), F32), pltpu.VMEM((STATE, INNER), F32)],
        compiler_params=pltpu.CompilerParams(dimension_semantics=("arbitrary",), vmem_limit_bytes=VMEM_BYTES),
        cost_estimate=pl.CostEstimate(flops=flops, bytes_accessed=30_000_000, transcendentals=0),
        name="ssd_forward",
    )(*ins)


def gate_kernel(
    keep_ref, normed_ref, ssd_ref, cot_ref, hidden_ref, wz_ref, wo_ref, gg_ref,
    out_ref, dz_ref, dssd_ref, no_ref, grow_ref, dgg_ref,
):
    @pl.when(pl.program_id(0) == 0)
    def _():
        dgg_ref[...] = jnp.zeros_like(dgg_ref)

    keep = keep_ref[:, 0:1]
    grow = (cot_ref[...].astype(F32) * keep).astype(BF16)
    grow_ref[...] = grow
    wo = wo_ref[...]
    gate_gain = gg_ref[...]
    z = mm(normed_ref[...], wz_ref[...])
    sig = sigmoid(z)
    silu = z * sig
    ssd = ssd_ref[...]
    gated = ssd * silu
    scale = lax.rsqrt(jnp.mean(gated * gated, axis=-1, keepdims=True) + EPS)
    unit = gated * scale
    out_low = (unit * gate_gain).astype(BF16)
    no_ref[...] = out_low
    out_ref[...] = (keep * (hidden_ref[...].astype(F32) + mm(out_low, wo))).astype(BF16)
    d_out = mm_bt(grow, wo)
    dgg_ref[...] += jnp.sum(d_out * unit, axis=0, keepdims=True)
    d_unit = d_out * gate_gain
    d_gated = scale * (d_unit - unit * jnp.mean(d_unit * unit, axis=-1, keepdims=True))
    dssd_ref[...] = d_gated * silu
    dz_ref[...] = (d_gated * ssd * (sig * (1.0 + z * (1.0 - sig)))).astype(BF16)


def gate(keep, normed, ssd, cot, hidden, wz, wo, gate_gain):
    rows, width = hidden.shape
    tile = 256
    whole = lambda a: pl.BlockSpec(a.shape, lambda i: (0,) * a.ndim)
    part = lambda n: pl.BlockSpec((tile, n), lambda i: (i, 0))
    return pl.pallas_call(
        gate_kernel,
        grid=(rows // tile,),
        in_specs=[part(LANES), part(width), part(INNER), part(width), part(width), whole(wz), whole(wo), whole(gate_gain)],
        out_specs=[part(width), part(INNER), part(INNER), part(INNER), part(width), pl.BlockSpec((1, INNER), lambda i: (0, 0))],
        out_shape=[
            jax.ShapeDtypeStruct((rows, width), BF16),
            jax.ShapeDtypeStruct((rows, INNER), BF16),
            jax.ShapeDtypeStruct((rows, INNER), F32),
            jax.ShapeDtypeStruct((rows, INNER), BF16),
            jax.ShapeDtypeStruct((rows, width), BF16),
            jax.ShapeDtypeStruct((1, INNER), F32),
        ],
        compiler_params=pltpu.CompilerParams(dimension_semantics=("arbitrary",), vmem_limit_bytes=VMEM_BYTES),
        cost_estimate=pl.CostEstimate(flops=2 * rows * width * INNER * 3, bytes_accessed=30_000_000, transcendentals=0),
        name="gate_both_ways",
    )(keep, normed, ssd, cot, hidden, wz, wo, gate_gain)


def backward_kernel(
    mixed_ref, slope_ref, convin_ref, step_ref, run_ref, sig_ref, ssd_ref, enter_ref, dssd_ref,
    cw_ref, alog_ref, skip_ref, spread_ref, gather_ref,
    dconv_ref, ddt_ref, dcw_ref, dcb_ref, dsmall_ref, dskip_ref,
    ahead, d_state, d_values,
):
    @pl.when(pl.program_id(0) == 0)
    def _():
        ahead[CHUNK : CHUNK + 8, :] = jnp.zeros((8, CHANNELS), F32)
        d_state[...] = jnp.zeros_like(d_state)
        dcw_ref[...] = jnp.zeros_like(dcw_ref)
        dcb_ref[...] = jnp.zeros_like(dcb_ref)
        dsmall_ref[...] = jnp.zeros_like(dsmall_ref)
        dskip_ref[...] = jnp.zeros_like(dskip_ref)

    spread = spread_ref[...]
    gather = gather_ref[...]
    step = step_ref[...]
    run = run_ref[...]
    run_t = jnp.transpose(run)
    last = run[CHUNK - 1 : CHUNK, :]
    skip = skip_ref[...]
    mixed = mixed_ref[...]
    values = mixed[:, :INNER].astype(F32)
    b_in = mixed[:, INNER : INNER + STATE]
    c_out = mixed[:, INNER + STATE :]
    step_wide = widen(step, spread)
    end_wide = widen(jnp.exp(last - run), spread)
    stepped = (step_wide * values).astype(BF16)
    to_end = (end_wide * stepped.astype(F32)).astype(BF16)
    through = widen(jnp.broadcast_to(jnp.exp(last), (8, LANES)), spread)[0:1, :]
    d_ssd = dssd_ref[...]
    d_low = d_ssd.astype(BF16)
    scaled = (widen(jnp.exp(run), spread) * d_low.astype(F32)).astype(BF16)
    entering = enter_ref[0]
    d_leave = d_state[...]
    d_leave_low = d_leave.astype(BF16)
    upper = triangle("upper")
    scores_t = jnp.where(upper, mm_bt(b_in, c_out), 0.0)

    left_half = lax.broadcasted_iota(jnp.int32, (CHUNK, LANES), 1) < HEAD_DIM
    zero = jnp.zeros((CHUNK, LANES), BF16)
    d_scores_t = jnp.zeros((CHUNK, CHUNK), F32)
    for pair in range(PAIRS):
        lanes = slice(pair * LANES, (pair + 1) * LANES)
        d_pair = d_low[:, lanes]
        x_pair = stepped[:, lanes]
        d_split = jnp.concatenate([jnp.where(left_half, d_pair, zero), jnp.where(left_half, zero, d_pair)], axis=0)
        d_mixing = mm_bt(x_pair, d_split)
        mixing = []
        for slot, h in enumerate((2 * pair, 2 * pair + 1)):
            decay = jnp.exp(jnp.minimum(run_t[h : h + 1, :] - run[:, h : h + 1], 0.0))
            d_scores_t = d_scores_t + d_mixing[:, slot * CHUNK : (slot + 1) * CHUNK] * decay
            mixing.append((scores_t * decay).astype(BF16))
        d_values[:, lanes] = mm(jnp.concatenate(mixing, axis=1), d_split)

    d_scores_t = jnp.where(upper, d_scores_t, 0.0).astype(BF16)
    d_c = mm_at(d_scores_t, b_in) + mm_bt(scaled, entering)
    d_b = mm(d_scores_t, c_out) + mm_bt(to_end, d_leave_low)
    from_state = mm(b_in, d_leave_low)
    d_state[...] = through * d_leave + mm_at(c_out, scaled)

    d_stepped = d_values[...]
    state_part = to_end.astype(F32) * from_state
    ssd = ssd_ref[...]
    flow = d_low.astype(F32) * (ssd - skip * values) - stepped.astype(F32) * d_stepped - state_part
    ending = jnp.sum(state_part, axis=0, keepdims=True) + through * jnp.sum(
        entering.astype(F32) * d_leave, axis=0, keepdims=True
    )
    is_last = lax.broadcasted_iota(jnp.int32, (CHUNK, 1), 0) == CHUNK - 1
    d_run = head_sums(flow + jnp.where(is_last, ending, 0.0), gather)
    d_stepped = d_stepped + end_wide * from_state
    d_step = head_sums(values * d_stepped, gather)
    dskip_ref[...] += jnp.sum(d_ssd * values, axis=0, keepdims=True)
    d_x = skip * d_ssd + step_wide * d_stepped

    rate = jnp.exp(alog_ref[...])
    d_log = jnp.dot(upper.astype(F32), d_run, precision=HIGHEST, preferred_element_type=F32)
    d_step = d_step - rate * d_log
    d_dt = jnp.where(lane_is_head(), d_step * sig_ref[...], 0.0)
    ddt_ref[...] = d_dt.astype(BF16)
    dsmall_ref[0:1, :] += jnp.sum(d_dt, axis=0, keepdims=True)
    dsmall_ref[1:2, :] -= rate * jnp.sum(d_log * step, axis=0, keepdims=True)

    slope = slope_ref[...].astype(F32)
    ahead[0:CHUNK, :INNER] = d_x * slope[:, :INNER]
    ahead[0:CHUNK, INNER : INNER + STATE] = d_b * slope[:, INNER : INNER + STATE]
    ahead[0:CHUNK, INNER + STATE :] = d_c * slope[:, INNER + STATE :]
    conv_in = convin_ref[...].astype(F32)
    total = jnp.zeros((CHUNK, CHANNELS), F32)
    for k in range(CONV_K):
        moved = ahead[CONV_K - 1 - k : CONV_K - 1 - k + CHUNK, :]
        total = total + cw_ref[k : k + 1, :] * moved
        dcw_ref[k : k + 1, :] += jnp.sum(moved * conv_in, axis=0, keepdims=True)
    dcb_ref[...] += jnp.sum(ahead[0:CHUNK, :], axis=0, keepdims=True)
    dconv_ref[...] = total.astype(BF16)
    ahead[CHUNK : CHUNK + 8, :] = ahead[0:8, :]


def backward(mixed, slope, convin, step, run, sig, ssd, enter, d_ssd, cw, alog, skip_wide, spread, gather):
    rows = mixed.shape[0]
    chunks = rows // CHUNK
    whole = lambda a: pl.BlockSpec(a.shape, lambda i: (0,) * a.ndim)
    part = lambda n: pl.BlockSpec((CHUNK, n), lambda i: (chunks - 1 - i, 0))
    total = lambda r, n: pl.BlockSpec((r, n), lambda i: (0, 0))
    flops = 2 * rows * (5 * STATE * INNER + CHUNK * INNER * 4)
    return pl.pallas_call(
        backward_kernel,
        grid=(chunks,),
        in_specs=[
            part(CHANNELS), part(CHANNELS), part(CHANNELS), part(LANES), part(LANES), part(LANES), part(INNER),
            pl.BlockSpec((1, STATE, INNER), lambda i: (chunks - 1 - i, 0, 0)), part(INNER),
        ] + [whole(a) for a in (cw, alog, skip_wide, spread, gather)],
        out_specs=[part(CHANNELS), part(LANES), total(CONV_K, CHANNELS), total(1, CHANNELS), total(8, LANES), total(1, INNER)],
        out_shape=[
            jax.ShapeDtypeStruct((rows, CHANNELS), BF16),
            jax.ShapeDtypeStruct((rows, LANES), BF16),
            jax.ShapeDtypeStruct((CONV_K, CHANNELS), F32),
            jax.ShapeDtypeStruct((1, CHANNELS), F32),
            jax.ShapeDtypeStruct((8, LANES), F32),
            jax.ShapeDtypeStruct((1, INNER), F32),
        ],
        scratch_shapes=[
            pltpu.VMEM((CHUNK + 8, CHANNELS), F32), pltpu.VMEM((STATE, INNER), F32), pltpu.VMEM((CHUNK, INNER), F32),
        ],
        compiler_params=pltpu.CompilerParams(dimension_semantics=("arbitrary",), vmem_limit_bytes=VMEM_BYTES),
        cost_estimate=pl.CostEstimate(flops=flops, bytes_accessed=40_000_000, transcendentals=0),
        name="ssd_backward",
    )(mixed, slope, convin, step, run, sig, ssd, enter, d_ssd, cw, alog, skip_wide, spread, gather)


def entry_kernel(hidden_ref, grow_ref, dz_ref, dconv_ref, ddt_ref, gain_ref, wz_ref, wc_ref, wdt_ref, gh_ref, dgain_ref):
    @pl.when(pl.program_id(0) == 0)
    def _():
        dgain_ref[...] = jnp.zeros_like(dgain_ref)

    x = hidden_ref[...].astype(F32)
    scale = lax.rsqrt(jnp.mean(x * x, axis=-1, keepdims=True) + EPS)
    unit = x * scale
    d_normed = mm_bt(dz_ref[...], wz_ref[...]) + mm_bt(dconv_ref[...], wc_ref[...]) + mm_bt(ddt_ref[...], wdt_ref[...])
    dgain_ref[...] += jnp.sum(d_normed * unit, axis=0, keepdims=True)
    d_unit = d_normed * gain_ref[...]
    d_x = scale * (d_unit - unit * jnp.mean(d_unit * unit, axis=-1, keepdims=True))
    gh_ref[...] = grow_ref[...].astype(F32) + d_x


def entry(hidden, grow, dz, dconv, ddt, gain, wz, wc, wdt):
    rows, width = hidden.shape
    tile = 256
    whole = lambda a: pl.BlockSpec(a.shape, lambda i: (0,) * a.ndim)
    part = lambda n: pl.BlockSpec((tile, n), lambda i: (i, 0))
    return pl.pallas_call(
        entry_kernel,
        grid=(rows // tile,),
        in_specs=[part(width), part(width), part(INNER), part(CHANNELS), part(LANES)] + [whole(a) for a in (gain, wz, wc, wdt)],
        out_specs=[part(width), pl.BlockSpec((1, width), lambda i: (0, 0))],
        out_shape=[jax.ShapeDtypeStruct((rows, width), F32), jax.ShapeDtypeStruct((1, width), F32)],
        compiler_params=pltpu.CompilerParams(dimension_semantics=("arbitrary",), vmem_limit_bytes=VMEM_BYTES),
        cost_estimate=pl.CostEstimate(flops=2 * rows * width * (INNER + CHANNELS + LANES), bytes_accessed=20_000_000, transcendentals=0),
        name="input_norm_backward",
    )(hidden, grow, dz, dconv, ddt, gain, wz, wc, wdt)


def pad_lanes(v):
    return jnp.pad(v, [(0, 0)] * (v.ndim - 1) + [(0, LANES - v.shape[-1])])


def head_maps():
    lane = jnp.arange(INNER)[None, :] // HEAD_DIM
    row = jnp.arange(LANES)[:, None]
    spread = (lane == row % 64).astype(BF16)
    gather = (lane == row).astype(BF16).T
    return spread, gather


def contract_rows(left, right):
    return lax.dot_general(left, right, (((0,), (0,)), ((), ())), preferred_element_type=F32)


def block(hidden, lengths, full_norm, full_in, full_conv, full_bias, dt_bias, a_log, skip, full_gate, full_out, cotangent):
    length = hidden.shape[0]
    spread, gather = head_maps()
    gain = full_norm.astype(F32)[None, :]
    wz = full_in[:, :INNER]
    wc = full_in[:, INNER : INNER + CHANNELS]
    wdt = pad_lanes(full_in[:, INNER + CHANNELS :])
    cw = full_conv.astype(F32)
    cb = full_bias.astype(F32)[None, :]
    dtb = pad_lanes(dt_bias[None, :])
    alog = pad_lanes(a_log[None, :])
    skip_wide = jnp.repeat(skip, HEAD_DIM)[None, :]
    keep = jnp.broadcast_to((jnp.arange(length) < lengths[0]).astype(F32)[:, None], (length, LANES))
    normed, mixed, slope, convin, step, run, sig, ssd, enter = forward(
        hidden, gain, wc, wdt, cw, cb, dtb, alog, skip_wide, spread
    )
    block_out, dz, d_ssd, out_low, grow, d_gate = gate(
        keep, normed, ssd, cotangent, hidden, wz, full_out, full_gate.astype(F32)[None, :]
    )
    d_out_w = contract_rows(out_low, grow)
    dconv, ddt, dcw, dcb, dsmall, dskip = backward(
        mixed, slope, convin, step, run, sig, ssd, enter, d_ssd, cw, alog, skip_wide, spread, gather
    )
    grad_hidden, d_gain = entry(hidden, grow, dz, dconv, ddt, gain, wz, wc, wdt)
    d_in_w = jnp.concatenate(
        [contract_rows(normed, dz), contract_rows(normed, dconv), contract_rows(normed, ddt)[:, :HEADS]], axis=1
    )
    d_skip = dskip.reshape(HEADS, HEAD_DIM).sum(1)
    return (block_out, grad_hidden, d_gain[0], d_in_w, dcw, dcb[0], dsmall[0, :HEADS], dsmall[1, :HEADS], d_skip, d_gate[0], d_out_w)


def local(hidden, lengths, norm_gain, in_w, conv_w, conv_b, dt_bias, a_log, skip, gate_gain, out_w, cotangent):
    full_norm, full_in, full_conv, full_bias, full_gate, full_out = (
        lax.all_gather(norm_gain, "fsdp", axis=0, tiled=True),
        lax.all_gather(in_w, "fsdp", axis=0, tiled=True),
        lax.all_gather(conv_w, "fsdp", axis=1, tiled=True),
        lax.all_gather(conv_b, "fsdp", axis=0, tiled=True),
        lax.all_gather(gate_gain, "fsdp", axis=0, tiled=True),
        lax.all_gather(out_w, "fsdp", axis=0, tiled=True),
    )
    outs = block(
        hidden, lengths, full_norm, full_in, full_conv, full_bias, dt_bias, a_log, skip, full_gate, full_out, cotangent
    )
    block_out, grad_hidden, d_gain, d_in, d_cw, d_cb, d_dtb, d_alog, d_skip, d_gate, d_out = outs
    scatter = functools.partial(lax.psum_scatter, axis_name="fsdp", tiled=True)
    head_sums = lax.psum((d_dtb, d_alog, d_skip), "fsdp")
    return (
        block_out, grad_hidden, scatter(d_gain, scatter_dimension=0), scatter(d_in, scatter_dimension=0),
        scatter(d_cw, scatter_dimension=1), scatter(d_cb, scatter_dimension=0), *head_sums,
        scatter(d_gate, scatter_dimension=0), scatter(d_out, scatter_dimension=0),
    )


def solution(mesh):
    rows, split, none = P("fsdp", None), P("fsdp"), P()
    columns = P(None, "fsdp")
    return jax.shard_map(
        local,
        mesh=mesh,
        in_specs=(rows, split, split, rows, columns, split, none, none, none, split, rows, rows),
        out_specs=(rows, rows, split, rows, columns, split, none, none, none, split, rows),
        check_vma=False,
    )
```

time: 636 us -> 426 us (0.67); the launches traced: 628 us -> 425 us
  matrix products: 182 us -> 18.3 us
  other arithmetic: 122 us -> 10.1 us
  Pallas kernels: 0 us -> 89.2 us
  local copies, waits for them, and re-layouts: 62.1 us -> 21.4 us
  waiting for transfers between devices: 124 us -> 148 us
    dot_general x16 -> x0, matrix products: 163 us -> none  [the longest x3 75.5 us: scan_heads(): jnp.einsum('cqsh,cshp->cqhp', mixing, value_rows, precision=precise)]
    pallas_call x0 -> x4, Pallas kernels: none -> 89.2 us  [the longest x1 37.4 us: backward(): pl.pallas_call(backward_kernel, grid=(chunks,), in_specs=[part(CHANNELS),...]
    reduce_sum x11 -> x1, other arithmetic: 41.1 us -> 0.12 us  [block(): d_skip = dskip.reshape(HEADS, HEAD_DIM).sum(1)]
    reshape x19 -> x1, local copies, waits for them, and re-layouts: 25.2 us -> 0.07 us  [block(): d_skip = dskip.reshape(HEADS, HEAD_DIM).sum(1)]
    unnamed x5, waiting for transfers between devices: 124 us -> 143 us
    another operation x5 -> x0, other arithmetic: 12.4 us -> none
    add_any x2 -> x0, other arithmetic: 12.4 us -> none  [the longest x1 12.3 us: front_piece(): padded[offset:offset + length]]
    add x5 -> x0, other arithmetic: 8.95 us -> none  [the longest x4 5.1 us: carry_state(): return (factor[:, None, None] * state_now + fresh_state, state_now)]
  transfers between devices with their start and end apart: 4 -> 4, of which waited for: 1 -> 2; matrix products, arithmetic and copies ran while one was open for 32% -> 10% of each run, Pallas kernels for 0% -> 17%
where the time goes in v1:
time: 426 us; the launch traced here: 425 us
  waiting for transfers between devices  148 us (35%)
  blocking collectives  123 us (29%)
  Pallas kernels  89.2 us (21%)
  local copies, waits for them, and re-layouts  21.4 us (5%)
  matrix products  18.3 us (4%)
  between operations  14.6 us (3%)
  other arithmetic  10.1 us (2%)
    unnamed x5, waiting for transfers between devices  143 us
    unnamed x2, blocking collectives  82 us
    all_gather x1, blocking collectives, local(): lax.all_gather(conv_w, 'fsdp', axis=1, tiled=True)  40.9 us
    pallas_call x1, Pallas kernels, backward(): pl.pallas_call(backward_kernel, grid=(chunks,), in_specs=[part(CHANNELS),...  37.4 us
    pallas_call x1, Pallas kernels, forward(): pl.pallas_call(forward_kernel, grid=(chunks,), in_specs=[part(width)] + [...  22.6 us
    dot_general x4, matrix products, contract_rows(): lax.dot_general(left, right, (((0,), (0,)), ((), ())), preferred_element_...  18.3 us
    pallas_call x1, Pallas kernels, gate(): pl.pallas_call(gate_kernel, grid=(rows // tile,), in_specs=[part(LANES),...  17.1 us
    pallas_call x1, Pallas kernels, entry(): pl.pallas_call(entry_kernel, grid=(rows // tile,), in_specs=[part(width),...  12.1 us
  transfers between devices with their start and end apart: 4, of which 2 were waited for; matrix products, arithmetic and copies ran while one was open for 10% of the time, Pallas kernels for 17%

profile of v1, /device:TPU:0, one launch (start us, length us, event | category | flops | bytes accessed | tf_op | source)
XLA Modules:
  0.0 425.2 jit_solution(14816716333710341917)
XLA Ops:
  7.2 0.0 all-gather.4.cloned.1.call-start
  7.2 0.7 all-gather.4.cloned.1.call-update
  7.9 0.0 all-gather.6.cloned.1.call-start
  8.0 0.7 all-gather.6.cloned.1.call-update
  8.7 0.0 reduce-scatter.6.cloned.1.call-start
  9.4 0.8 dynamic-update-slice
  10.2 0.8 dynamic-update-slice.1
  11.1 0.8 dynamic-update-slice.2
  11.9 42.3 %all-reduce.12 = (bf16[768]{0:T(1024)(128)(2,1)S(1)}, bf16[1792]{0:T(1024)(128)(2,1)S(1)}, bf16[1536]{0:T(1024)(128)(2,1)S(1)}) all-reduce(bf16[768]{0:T(1024)(128)(2,1)S(1)} %dynamic-update-slice, bf16[1792]{0:T(1024)(128)(2,1)S(1)} %dynamic-update-slice.1, bf16[1536]{0:T(1024)(128)(2,1)S(1)} %dynamic-update-slice.2), channel_id=1, replica_groups=mesh['fsdp'=32] {'fsdp'}, use_global_device_ids=true, to_apply=%add.3 | all-reduce | flops 4096 | bytes 16384
  54.2 0.6 reshape.83.gain_ref
  54.8 40.9 %all-gather = bf16[32,56,4]{1,2,0:T(4,128)(2,1)S(1)} all-gather(bf16[1,56,4]{1,2,0:T(4,128)(2,1)} %bitcast.25), channel_id=1, replica_groups=mesh['fsdp'=32] {'fsdp'}, dimensions={0}, use_global_device_ids=true | all-gather | bytes 14784 | tf_op jit(solution)/shard_map/all_gather | solution.py:437
  95.7 0.7 reshape.94
  96.4 0.6 reshape.84.cb_ref
  97.0 1.2 pad.12.dtb_ref
  98.2 1.2 pad.13.alog_ref
  99.3 0.7 broadcast_in_dim.39
  100.1 0.7 broadcast_in_dim_reshape.3.skip_ref
  100.8 0.6 reshape.85.gg_ref
  101.4 0.9 compare_convert_fusion.spread_ref
  102.3 0.0 all-gather.4.cloned.1.call-done
  102.3 0.9 slice.26
  103.2 0.7 pad.11.wdt_ref
  103.9 3.5 slice.25.wc_ref
  107.4 3.2 slice.27.wz_ref
  110.6 22.6 %ssd_forward.1 = (bf16[1024,768]{1,0:T(8,128)(2,1)}, bf16[1024,1792]{1,0:T(8,128)(2,1)}, bf16[1024,1792]{1,0:T(8,128)(2,1)}, bf16[1024,1792]{1,0:T(8,128)(2,1)},...) custom-call(bf16[1024,768]{1,0:T(8,128)(2,1)} %hidden_ref.5, ...), custom_call_target="tpu_custom_call" | custom-call | flops 5033164800 | bytes 30000000 | tf_op jit(solution)/shard_map/ssd_forward/pallas_call | solution.py:142
  133.2 5.4 %all-gather.6.cloned.1.call-done.wo_ref = bf16[1536,768]{1,0:T(8,128)(2,1)} async-done(((bf16[48,768]{1,0:T(8,128)(2,1)}), bf16[1536,768]{1,0:T(8,128)(2,1)}) %all-gather.6.cloned.1.call-update) | async-done | bytes 2359312 | tf_op jit(solution)/shard_map/all_gather | solution.py:440
  138.5 1.0 broadcast_in_dim.32.keep_ref
  139.6 17.1 %gate_both_ways.1 = (bf16[1024,768]{1,0:T(8,128)(2,1)}, bf16[1024,1536]{1,0:T(8,128)(2,1)}, f32[1024,1536]{1,0:T(8,128)}, bf16[1024,1536]{1,0:T(8,128)(2,1)}, bf...) custom-call(f32[1024,128]{1,0:T(8,128)} %broadcast_in_dim.32.keep_ref, bf16[1024,768]{1,0:T(8,128)(2,1)} %get-tuple-element.34.normed_ref, ...), custom_call_target="tpu_custom_call" | custom-call | flops 7247757312 | bytes 30000000 | tf_op jit(solution)/shard_map/gate_both_ways/pallas_call | solution.py:204
  156.7 7.1 %fusion.9 = f32[1536,768]{1,0:T(8,128)} fusion(bf16[1024,1536]{1,0:T(8,128)(2,1)} %get-tuple-element.56, bf16[1024,768]{1,0:T(8,128)(2,1)} %get-tuple-element.37.grow_ref), kind=kOutput, calls=%fused_computation.22 | convolution fusion | flops 2415919104 | bytes 9437184 | tf_op jit(solution)/shard_map/dot_general | solution.py:399
  163.8 0.0 reduce-scatter.6.cloned.1.call-update
  163.8 0.2 reduce-scatter.8.cloned.1.call-start
  164.1 1.0 fusion.gather_ref
  165.1 0.0 copy-start
  165.1 37.4 %ssd_backward.1 = (bf16[1024,1792]{1,0:T(8,128)(2,1)}, bf16[1024,128]{1,0:T(8,128)(2,1)}, f32[4,1792]{1,0:T(4,128)}, f32[1,1792]{1,0:T(1,128)}, f32[8,128]{1,0:T(8,128)}, /*index=5*/f32[1,1536]{1,0:T(1,128)}) custom-call(bf16[1024,1792]{1,0:T(8,128)(2,1)} %get-tuple-element.39.mixed_ref, bf16[1024,1792]{1,0:T(8,128)(2,1)} %get-tuple-element.40.slope_ref, ...), custom_call_target="tpu_custom_call" | custom-call | flops 3623878656 | bytes 40000000 | tf_op jit(solution)/shard_map/ssd_backward/pallas_call | solution.py:329
  202.6 0.0 copy-done
  202.6 1.6 fusion.1
  204.1 0.0 copy-start.1
  204.1 4.7 %fusion.7 = f32[768,1536]{1,0:T(8,128)S(1)} fusion(bf16[1024,768]{1,0:T(8,128)(2,1)S(1)} %copy-done, bf16[1024,1536]{1,0:T(8,128)(2,1)} %get-tuple-element.38.dz_ref), kind=kOutput, calls=%fused_computation.20 | convolution fusion | flops 2415919104 | bytes 9437184 | tf_op jit(solution)/shard_map/dot_general | solution.py:399
  208.9 0.0 copy-done.1
  208.9 4.9 %fusion.8 = f32[768,1792]{1,0:T(8,128)} fusion(bf16[1024,768]{1,0:T(8,128)(2,1)S(1)} %copy-done, bf16[1024,1792]{1,0:T(8,128)(2,1)S(1)} %copy-done.1), kind=kOutput, calls=%fused_computation.21 | convolution fusion | flops 2818572288 | bytes 10747904 | tf_op jit(solution)/shard_map/dot_general | solution.py:399
  213.7 7.3 %pad_maximum_fusion = f32[768,3352]{1,0:T(8,128)} fusion(f32[768,24]{1,0:T(8,128)S(1)} %fusion.1, f32[768,1792]{1,0:T(8,128)} %fusion.8, f32[768,1536]{1,0:T(8,128)S(1)} %fusion.7), kind=kLoop, calls=%fused_computation | loop fusion | flops 5148672 | bytes 20594688 | tf_op jit(solution)/shard_map/concatenate | solution.py:426
  221.0 0.0 reduce-scatter.8.cloned.1.call-update
  221.0 0.0 copy-start.3
  221.1 0.0 copy-start.5
  221.1 0.0 copy-start.4
  221.1 0.0 copy-start.2
  221.1 12.1 %input_norm_backward.1 = (f32[1024,768]{1,0:T(8,128)}, f32[1,768]{1,0:T(1,128)}) custom-call(bf16[1024,768]{1,0:T(8,128)(2,1)} %hidden_ref.5, bf16[1024,768]{1,0:T(8,128)(2,1)} %get-tuple-element.37.grow_ref, bf16[1024,1536]{1,0:T(8,128)(2,1)} %get-tuple-element.38.dz_ref, bf16[1024,1792]{1,0:T(8,128)(2,1)} %get-tuple-element.47.dconv_ref, ...), custom_call_target="tpu_custom_call" | custom-call | flops 5435817984 | bytes 20000000 | tf_op jit(solution)/shard_map/input_norm_backward/pallas_call | solution.py:374
  233.2 0.7 reduce
  233.9 0.0 copy-done.3
  233.9 0.0 copy-done.5
  233.9 0.1 reshape.82
  234.0 0.1 reduce_sum.9
  234.1 0.0 copy-done.4
  234.2 0.8 slice_bitcast_fusion
  234.9 0.0 copy-done.2
  234.9 39.7 %all-reduce.11 = (f32[768]{0:T(1024)S(1)}, f32[4,1792]{1,0:T(4,128)S(1)}, f32[1792]{0:T(1024)S(1)}, f32[24]{0:T(128)}, f32[24]{0:T(128)}, /*index=5*/f32[24]{0:T(128)}, f32[1536]{0:T(1024)S(1)}) all-reduce(f32[768]{0:T(1024)S(1)} %reduce, f32[4,1792]{1,0:T(4,128)S(1)} %copy-done.2, ...), channel_id=2, replica_groups=mesh['fsdp'=32] {'fsdp'}, use_global_device_ids=true, to_apply=%region_0.1.clone | all-reduce | flops 11336 | bytes 90688
  274.7 0.6 dynamic-slice
  275.2 0.6 dynamic-slice.3
  275.8 0.6 dynamic-slice.4
  276.4 0.6 constant_dynamic-slice_fusion
  277.1 0.0 reduce-scatter.6.cloned.1.call-done
  277.1 141.6 %reduce-scatter.8.cloned.1.call-done = f32[24,3352]{1,0:T(8,128)} async-done(((f32[768,3352]{1,0:T(8,128)}), f32[24,3352]{1,0:T(8,128)}) %reduce-scatter.8.cloned.1.call-update) | async-done | bytes 321808
  (10 shorter events, 0.1 us)
Async XLA Ops:
  7.2 95.1 %all-gather.4.cloned.1.call-start = ((), (), s32[]{:S(2)}) async-start(), calls=%async_computation.2 | async-start | bytes 5474304 | tf_op jit(solution)/shard_map/all_gather | solution.py:436
  7.9 130.6 %all-gather.6.cloned.1.call-start = ((), (), s32[]{:S(2)}) async-start(), calls=%async_computation.3 | async-start | bytes 2433024 | tf_op jit(solution)/shard_map/all_gather | solution.py:440
  8.7 268.4 %reduce-scatter.6.cloned.1.call-start = ((), (), s32[]{:S(2)}) async-start(), calls=%async_computation.4 | async-start | bytes 4866048 | tf_op jit(solution)/shard_map/reduce_scatter | solution.py:451
  163.8 254.8 %reduce-scatter.8.cloned.1.call-start = ((), (), s32[]{:S(2)}) async-start(), calls=%async_computation.5 | async-start | bytes 10948608
  165.1 37.5 %copy-start = (bf16[1024,768]{1,0:T(8,128)(2,1)S(1)}, bf16[1024,768]{1,0:T(8,128)(2,1)}, u32[]{:S(2)}) copy-start(bf16[1024,768]{1,0:T(8,128)(2,1)} %get-tuple-element.34.normed_ref) | copy-start | bytes 4718596
  204.1 4.7 %copy-start.1 = (bf16[1024,1792]{1,0:T(8,128)(2,1)S(1)}, bf16[1024,1792]{1,0:T(8,128)(2,1)}, u32[]{:S(2)}) copy-start(bf16[1024,1792]{1,0:T(8,128)(2,1)} %get-tuple-element.47.dconv_ref) | copy-start | bytes 11010052
  221.0 12.8 %copy-start.3 = (f32[1,1792]{1,0:T(1,128)S(1)}, f32[1,1792]{1,0:T(1,128)}, u32[]{:S(2)}) copy-start(f32[1,1792]{1,0:T(1,128)} %get-tuple-element.52) | copy-start | bytes 21508
  221.1 12.8 %copy-start.5 = (f32[1,1536]{1,0:T(1,128)S(1)}, f32[1,1536]{1,0:T(1,128)}, u32[]{:S(2)}) copy-start(f32[1,1536]{1,0:T(1,128)} %get-tuple-element.54) | copy-start | bytes 18436
  221.1 13.1 %copy-start.4 = (f32[1,1536]{1,0:T(1,128)S(1)}, f32[1,1536]{1,0:T(1,128)}, u32[]{:S(2)}) copy-start(f32[1,1536]{1,0:T(1,128)} %get-tuple-element.55) | copy-start | bytes 18436
  221.1 13.8 %copy-start.2 = (f32[4,1792]{1,0:T(4,128)S(1)}, f32[4,1792]{1,0:T(4,128)}, u32[]{:S(2)}) copy-start(f32[4,1792]{1,0:T(4,128)} %get-tuple-element.51) | copy-start | bytes 86020
Sparse Core Ops, SparseCore 0:
  10.9 68.5 all-gather.3
  82.4 56.0 all-gather.5
  163.9 106.3 reduce-scatter.5
  277.9 140.6 reduce-scatter.7
